TPU v7x, 512 devices: a whole 4x8x8 slice. The times are simulated.
512 devices in a mesh: section: 4 (over x), ed: 64 (over y, z), tp: 2 (over core).
Axes of the slice: x: 4, y: 8, z: 8, core: 2. Of those that a mesh axis runs over, the one named last changes fastest.
Arguments:
- top_cotangent: bfloat16 [4, 2048, 3072], P(None, 'ed', 'tp'), may hold values from -6 to 6
- layer_inputs: bfloat16 [4, 4, 2048, 3072], P('section', None, 'ed', 'tp'), may hold values from -16 to 16
- router_weight: float32 [4, 3072, 8], P('section'), may hold values from -0.109375 to 0.109375
- expert_ids: int32 [4, 4, 2048, 2], P('section', None, 'ed'), may hold values from 0 to 7, all different within a row; in each aligned block of 32 rows (0 to 31, 32 to 63, ..., all dimensions but the last counted through in order) at most 12 rows name the same one
- expert_outputs: bfloat16 [4, 4, 2048, 2, 3072], P('section', None, 'ed', None, 'tp'), may hold values from -1.5 to 1.5
- hidden: bfloat16 [4, 4, 2048, 2, 8192], P('section', None, 'ed', None, 'tp'), may hold values from -6 to 6
Outputs:
- section_cotangents: bfloat16 [4, 4, 2048, 3072], P('section', None, 'ed', 'tp')
- down_grad: bfloat16 [4, 2, 64, 512, 1536], P('section', 'tp', 'ed')
- router_grad: float32 [4, 2, 1536, 8], P('section', 'tp', 'ed')
Inputs may be any that keep to these rules, and one draw needn't show every extreme that they name: `expert_ids`: each token names two different experts. In every layer, micro-batch and index of ed (each aligned block of 32 tokens) no expert is named by more than 12 tokens, a bound that some block reaches.
All inputs are finite; a program needn't handle non-finite values.
Results may differ from a plain program's by a relative error of at most 0.0062.
Values may be sent and summed in bfloat16 or wider, within the bound.
A program may use at most 128 MiB of HBM per device.

v0:
```python
import jax
import jax.numpy as jnp
from jax import lax
from jax.sharding import PartitionSpec as P

CAP = 12


def from_behind(shard, axis, by):
    count = lax.axis_size(axis)
    pairs = [(i, i + by) for i in range(count) if 0 <= i + by < count]
    return lax.ppermute(shard, axis, pairs)


def per_device(top_cotangent, layer_inputs, router_weight, expert_ids, expert_outputs, hidden):
    n_section = lax.axis_size("section")
    n_ed = lax.axis_size("ed")
    section = lax.axis_index("section")
    core = lax.axis_index("tp")
    micro, tok, half_d = top_cotangent.shape
    width = router_weight.shape[1]
    experts = router_weight.shape[2]
    half_ff = hidden.shape[4]
    routes = tok * 2
    slots = CAP
    window = min(4, n_ed // 2)
    row_blocks = n_ed // (2 * window)
    tile_rows = half_ff // row_blocks
    top_full = lax.all_gather(top_cotangent, "tp", axis=2, tiled=True)
    inputs_half = layer_inputs[0].astype(jnp.float32)
    weights = router_weight[0]
    weights_half = lax.dynamic_slice_in_dim(weights, core * half_d, half_d, 0)
    ids = expert_ids[0]
    saved_out = expert_outputs[0]
    saved_hidden = hidden[0]
    partial_logits = jnp.einsum(
        "mtd,de->mte", inputs_half, weights_half, precision=lax.Precision.HIGHEST
    )
    logits = lax.psum(partial_logits, "tp")
    iota_e = jnp.arange(experts, dtype=jnp.int32)
    onehot = (ids[..., None] == iota_e).astype(jnp.float32)
    picked = jnp.sum(onehot * logits[:, :, None, :], axis=-1)
    first = 1.0 / (1.0 + jnp.exp(picked[..., 1] - picked[..., 0]))
    gates = jnp.stack([first, 1.0 - first], axis=-1)
    select = onehot[:, :, 0, :] - onehot[:, :, 1, :]
    flat_hot = onehot.reshape(micro, routes, experts)[:, :, :window]
    rank = jnp.sum((jnp.cumsum(flat_hot, axis=1) - 1.0) * flat_hot, axis=-1)
    slot_iota = jnp.arange(slots, dtype=jnp.float32)
    place = (
        jnp.transpose(flat_hot, (0, 2, 1))[:, :, None, :]
        * (rank[:, None, None, :] == slot_iota[None, None, :, None]).astype(jnp.float32)
    ).astype(jnp.bfloat16)
    carried = jnp.zeros((tok, width), jnp.bfloat16)
    cot_out = jnp.zeros((micro, tok, half_d), jnp.bfloat16)
    router_part = jnp.zeros((half_d, experts), jnp.float32)
    grad_tile = jnp.zeros((tile_rows, half_d), jnp.float32)
    saved_scaled = jnp.zeros((micro, tok, 2, width), jnp.bfloat16)
    for tick in range(micro + n_section - 1):
        m_index = tick - (n_section - 1) + section
        active = (m_index >= 0) & (m_index < micro)
        m_safe = jnp.clip(m_index, 0, micro - 1)
        entry = lax.dynamic_index_in_dim(top_full, m_safe, 0, keepdims=False)
        upstream = jnp.where(section == n_section - 1, entry, carried)
        up32 = upstream.astype(jnp.float32)
        own_half = lax.dynamic_slice_in_dim(upstream, core * half_d, half_d, 1)
        out_now = lax.dynamic_index_in_dim(saved_out, m_safe, 0, keepdims=False)
        partial_dots = jnp.einsum(
            "td,tkd->tk", own_half, out_now, preferred_element_type=jnp.float32
        )
        gate_grad = lax.psum(partial_dots, "tp")
        gates_now = lax.dynamic_index_in_dim(gates, m_safe, 0, keepdims=False)
        first_now = gates_now[:, 0]
        logit_grad = first_now * (1.0 - first_now) * (gate_grad[:, 0] - gate_grad[:, 1])
        dlogits = logit_grad[:, None] * lax.dynamic_index_in_dim(select, m_safe, 0, keepdims=False)
        cotangent = (up32 + jnp.dot(dlogits, weights.T, precision=lax.Precision.HIGHEST)).astype(
            jnp.bfloat16
        )
        cot_half = lax.dynamic_slice_in_dim(cotangent, core * half_d, half_d, 1)
        cot_out = jnp.where(
            active, lax.dynamic_update_index_in_dim(cot_out, cot_half, m_safe, 0), cot_out
        )
        inputs_now = lax.dynamic_index_in_dim(inputs_half, m_safe, 0, keepdims=False)
        router_term = jnp.dot(inputs_now.T, dlogits, precision=lax.Precision.HIGHEST)
        router_part = router_part + jnp.where(active, router_term, 0.0)
        scaled = (gates_now[:, :, None] * up32[:, None, :]).astype(jnp.bfloat16)
        saved_scaled = jnp.where(
            active, lax.dynamic_update_index_in_dim(saved_scaled, scaled, m_safe, 0), saved_scaled
        )
        if tick >= n_section - 1:
            m_done = tick - (n_section - 1)
            place_now = place[m_done]
            hidden_now = saved_hidden[m_done].reshape(routes, half_ff)
            hidden_slots = jnp.einsum(
                "ecr,rf->ecf", place_now, hidden_now, preferred_element_type=jnp.float32
            ).astype(jnp.bfloat16)
            hidden_slots = hidden_slots.reshape(window, slots, row_blocks, tile_rows).transpose(
                0, 2, 1, 3
            )
            hidden_slots = jnp.broadcast_to(
                hidden_slots[:, :, None], (window, row_blocks, 2, slots, tile_rows)
            ).reshape(n_ed, slots, tile_rows)
            scaled_slots = jnp.einsum(
                "ecr,rd->ecd",
                place_now,
                saved_scaled[m_done].reshape(routes, width),
                preferred_element_type=jnp.float32,
            ).astype(jnp.bfloat16)
            scaled_slots = scaled_slots.reshape(window, slots, 2, half_d).transpose(0, 2, 1, 3)
            scaled_slots = jnp.broadcast_to(
                scaled_slots[:, None], (window, row_blocks, 2, slots, half_d)
            ).reshape(n_ed, slots, half_d)
            hidden_slots, scaled_slots = (hidden_slots, scaled_slots)
            got_hidden, got_scaled = (
                lax.all_to_all(hidden_slots, "ed", split_axis=0, concat_axis=0, tiled=True),
                lax.all_to_all(scaled_slots, "ed", split_axis=0, concat_axis=0, tiled=True),
            )
            grad_tile = grad_tile + jnp.einsum(
                "scf,scd->fd", got_hidden, got_scaled, preferred_element_type=jnp.float32
            )
        carried = from_behind(cotangent, "section", -1)
    down = grad_tile.astype(jnp.bfloat16).reshape(1, 1, 1, tile_rows, half_d)
    router = lax.psum_scatter(router_part, "ed", scatter_dimension=0, tiled=True)
    return (cot_out[None], down, router.reshape(1, 1, half_d // n_ed, experts))


def solution(mesh):
    in_specs = (
        P(None, "ed", "tp"),
        P("section", None, "ed", "tp"),
        P("section", None, None),
        P("section", None, "ed", None),
        P("section", None, "ed", None, "tp"),
        P("section", None, "ed", None, "tp"),
    )
    out_specs = (
        P("section", None, "ed", "tp"),
        P("section", "tp", "ed", None, None),
        P("section", "tp", "ed", None),
    )
    return jax.shard_map(
        per_device, mesh=mesh, in_specs=in_specs, out_specs=out_specs, check_vma=False
    )
```

profile of v0, /device:TPU:36, one launch (start us, length us, event | category | flops | bytes accessed | tf_op | source)
XLA Modules:
  0.0 898.7 jit_solution(12673897199588445563)
XLA Ops:
  0.7 2.7 all_gather.3
  6.4 3.4 all-reduce.1
  11.1 2.4 collective-permute-start
  14.9 4.3 fusion.186
  22.0 16.5 %all-to-all-start.2 = ((bf16[64,12,512]{2,1,0:T(8,128)(2,1)}), bf16[64,12,512]{2,1,0:T(8,128)(2,1)}, u32[]{:S(2)}, u32[]{:S(2)}) async-start(bf16[64,12,512]{2,1,0:T(8,128)(2,1)} %bitcast.86), calls=%async_computation.2 | async-start | bytes 2097152 | tf_op jit(solution)/shard_map/all_to_all | solution.py:114
  48.2 1.4 fusion.25
  50.7 2.1 reshape.381
  52.8 1.9 copy.111
  54.7 1.7 fusion.184
  57.6 1.3 copy.120
  58.9 3.1 psum.58
  63.2 2.5 collective-permute-start.1
  65.7 1.5 fusion.26
  67.2 4.9 collective-permute-done.1
  75.4 3.1 psum.59
  79.7 2.1 broadcast_in_dim.138
  81.8 18.3 %all-to-all-start = ((bf16[64,12,512]{2,1,0:T(8,128)(2,1)}), bf16[64,12,512]{2,1,0:T(8,128)(2,1)}, u32[]{:S(2)}, u32[]{:S(2)}) async-start(bf16[64,12,512]{2,1,0:T(8,128)(2,1)} %bitcast.342), calls=%async_computation | async-start | bytes 2097152 | tf_op jit(solution)/shard_map/all_to_all | solution.py:114
  101.3 2.4 collective-permute-start.2
  103.8 1.5 fusion.27
  105.3 4.6 collective-permute-done.2
  110.7 17.5 %all-to-all-done = bf16[64,12,512]{2,1,0:T(8,128)(2,1)} async-done(((bf16[64,12,512]{2,1,0:T(8,128)(2,1)}), bf16[64,12,512]{2,1,0:T(8,128)(2,1)}, u32[]{:S(2)}, u32[]{:S(2)}) %all-to-all-start) | async-done | bytes 786464 | tf_op jit(solution)/shard_map/all_to_all | solution.py:114
  128.2 2.1 broadcast_in_dim.144
  130.3 9.3 %all-to-all-start.4 = ((bf16[64,12,512]{2,1,0:T(8,128)(2,1)}), bf16[64,12,512]{2,1,0:T(8,128)(2,1)}, u32[]{:S(2)}, u32[]{:S(2)}) async-start(bf16[64,12,512]{2,1,0:T(8,128)(2,1)} %bitcast.340), calls=%async_computation.4 | async-start | bytes 2097152 | tf_op jit(solution)/shard_map/all_to_all | solution.py:114
  140.8 1.4 copy.124
  142.2 3.2 psum.60
  147.3 2.4 collective-permute-start.3
  149.7 1.5 fusion.28
  151.3 15.2 %all-to-all-done.4 = bf16[64,12,512]{2,1,0:T(8,128)(2,1)} async-done(((bf16[64,12,512]{2,1,0:T(8,128)(2,1)}), bf16[64,12,512]{2,1,0:T(8,128)(2,1)}, u32[]{:S(2)}, u32[]{:S(2)}) %all-to-all-start.4) | async-done | bytes 786464 | tf_op jit(solution)/shard_map/all_to_all | solution.py:114
  166.4 2.1 broadcast_in_dim.146
  168.6 8.7 all-to-all-start.6
  178.3 1.6 fusion.187
  179.9 1.9 reshape.357
  181.8 2.0 convolution_convert_fusion.7
  183.7 1.9 reshape.371
  185.6 1.7 copy.93
  187.4 17.0 %all-to-all-done.6 = bf16[64,12,512]{2,1,0:T(8,128)(2,1)} async-done(((bf16[64,12,512]{2,1,0:T(8,128)(2,1)}), bf16[64,12,512]{2,1,0:T(8,128)(2,1)}, u32[]{:S(2)}, u32[]{:S(2)}) %all-to-all-start.6) | async-done | bytes 786464 | tf_op jit(solution)/shard_map/all_to_all | solution.py:114
  204.3 3.1 broadcast_in_dim.141
  207.4 8.8 all-to-all-start.1
  216.9 2.5 psum.61
  220.5 2.4 collective-permute-start.4
  223.1 6.6 collective-permute-done.4
  230.7 1.6 fusion.30
  232.3 1.9 reshape.360
  234.2 2.0 convolution_convert_fusion.6
  236.1 1.9 reshape.375
  238.0 1.7 copy.100
  239.8 57.1 %all-to-all-done.1 = bf16[64,12,1536]{2,1,0:T(8,128)(2,1)} async-done(((bf16[64,12,1536]{2,1,0:T(8,128)(2,1)}), bf16[64,12,1536]{2,1,0:T(8,128)(2,1)}, u32[]{:S(2)}, u32[]{:S(2)}) %all-to-all-start.1) | async-done | bytes 2359328 | tf_op jit(solution)/shard_map/all_to_all | solution.py:115
  296.8 3.1 broadcast_in_dim.143
  299.9 23.2 %all-to-all-start.3 = ((bf16[64,12,1536]{2,1,0:T(8,128)(2,1)}), bf16[64,12,1536]{2,1,0:T(8,128)(2,1)}, u32[]{:S(2)}, u32[]{:S(2)}) async-start(bf16[64,12,1536]{2,1,0:T(8,128)(2,1)} %bitcast.338), calls=%async_computation.3 | async-start | bytes 6291456 | tf_op jit(solution)/shard_map/all_to_all | solution.py:115
  323.8 2.5 psum.62
  327.5 2.4 collective-permute-start.5
  330.0 6.5 collective-permute-done.5
  338.7 61.0 %all-to-all-done.3 = bf16[64,12,1536]{2,1,0:T(8,128)(2,1)} async-done(((bf16[64,12,1536]{2,1,0:T(8,128)(2,1)}), bf16[64,12,1536]{2,1,0:T(8,128)(2,1)}, u32[]{:S(2)}, u32[]{:S(2)}) %all-to-all-start.3) | async-done | bytes 2359328 | tf_op jit(solution)/shard_map/all_to_all | solution.py:115
  399.7 2.1 broadcast_in_dim.145
  401.7 23.8 %all-to-all-start.5 = ((bf16[64,12,1536]{2,1,0:T(8,128)(2,1)}), bf16[64,12,1536]{2,1,0:T(8,128)(2,1)}, u32[]{:S(2)}, u32[]{:S(2)}) async-start(bf16[64,12,1536]{2,1,0:T(8,128)(2,1)} %bitcast.337), calls=%async_computation.5 | async-start | bytes 6291456 | tf_op jit(solution)/shard_map/all_to_all | solution.py:115
  433.6 66.8 %all-to-all-done.5 = bf16[64,12,1536]{2,1,0:T(8,128)(2,1)} async-done(((bf16[64,12,1536]{2,1,0:T(8,128)(2,1)}), bf16[64,12,1536]{2,1,0:T(8,128)(2,1)}, u32[]{:S(2)}, u32[]{:S(2)}) %all-to-all-start.5) | async-done | bytes 2359328 | tf_op jit(solution)/shard_map/all_to_all | solution.py:115
  500.3 2.0 broadcast_in_dim.147
  502.4 21.9 %all-to-all-start.7 = ((bf16[64,12,1536]{2,1,0:T(8,128)(2,1)}), bf16[64,12,1536]{2,1,0:T(8,128)(2,1)}, u32[]{:S(2)}, u32[]{:S(2)}) async-start(bf16[64,12,1536]{2,1,0:T(8,128)(2,1)} %bitcast.335), calls=%async_computation.7 | async-start | bytes 6291456 | tf_op jit(solution)/shard_map/all_to_all | solution.py:115
  527.2 2.5 psum.63
  530.0 338.8 %all-reduce = f32[1536,8]{0,1:T(8,128)S(1)} all-reduce(f32[1536,8]{0,1:T(8,128)S(1)} %fusion.20), channel_id=2, replica_groups=mesh['section'=4,'ed'=64,'tp'=2] {'ed'}, use_global_device_ids=true, to_apply=%region_11.12.clone | all-reduce | flops 12288 | bytes 98304
  870.1 6.1 convolution_bitcast_fusion.2
  876.2 6.0 fusion.6
  882.3 7.7 fusion.7
  890.0 8.3 fusion.10
  (175 shorter events, 50.4 us)
Async XLA Ops:
  0.6 4.3 copy-start
  0.6 9.2 %copy-start.13 = (s32[1,4,32,2]{2,3,1,0:T(2,128)S(1)}, s32[1,4,32,2]{2,3,1,0:T(2,128)}, u32[]{:S(2)}) copy-start(s32[1,4,32,2]{2,3,1,0:T(2,128)} %param.9) | copy-start | bytes 3076
  0.7 4.9 copy-start.1
  0.7 4.9 copy-start.2
  9.9 9.3 %copy-start.14 = (f32[4,32,1]{1,2,0:T(1,128)}, f32[4,32,1]{1,2,0:T(1,128)S(1)}, u32[]{:S(2)}) copy-start(f32[4,32,1]{1,2,0:T(1,128)S(1)} %get-tuple-element.19) | copy-start | bytes 1540
  9.9 9.3 %copy-start.16 = (f32[4,32,1]{1,2,0:T(1,128)}, f32[4,32,1]{1,2,0:T(1,128)S(1)}, u32[]{:S(2)}) copy-start(f32[4,32,1]{1,2,0:T(1,128)S(1)} %get-tuple-element.20) | copy-start | bytes 1540
  10.5 3.3 copy-start.24
  10.5 8.7 copy-start.26
  11.1 8.2 copy-start.7
  11.1 43.6 %collective-permute-start = (bf16[32,3072]{1,0:T(8,128)(2,1)S(1)}, bf16[32,3072]{1,0:T(8,128)(2,1)}, u32[]{:S(2)}, u32[]{:S(2)}) collective-permute-start(bf16[32,3072]{1,0:T(8,128)(2,1)S(1)} %fusion), channel_id=1, source_target_pairs={{128,0},{256,128},{384,256},{129,1},{257,129},{385,257},{130,2},{2... | collective-permute-start | bytes 589832 | tf_op jit(solution)/shard_map/ppermute | solution.py:12
  20.7 17.9 %copy-start.25 = (f32[32,2]{0,1:T(2,128)S(1)}, f32[32,2]{0,1:T(2,128)}, u32[]{:S(2)}) copy-start(f32[32,2]{0,1:T(2,128)} %copy-done.24) | copy-start | bytes 772
  20.7 18.6 %copy-start.23 = (f32[32,2]{0,1:T(2,128)S(1)}, f32[32,2]{0,1:T(2,128)}, u32[]{:S(2)}) copy-start(f32[32,2]{0,1:T(2,128)} %get-tuple-element.33) | copy-start | bytes 772
  20.8 19.2 %copy-start.22 = (f32[32,2]{0,1:T(2,128)S(1)}, f32[32,2]{0,1:T(2,128)}, u32[]{:S(2)}) copy-start(f32[32,2]{0,1:T(2,128)} %get-tuple-element.34) | copy-start | bytes 772
  20.8 19.9 %copy-start.21 = (f32[32,2]{0,1:T(2,128)S(1)}, f32[32,2]{0,1:T(2,128)}, u32[]{:S(2)}) copy-start(f32[32,2]{0,1:T(2,128)} %get-tuple-element.35) | copy-start | bytes 772
  20.8 20.0 %copy-start.19 = (f32[32,2]{0,1:T(2,128)S(1)}, f32[32,2]{0,1:T(2,128)}, u32[]{:S(2)}) copy-start(f32[32,2]{0,1:T(2,128)} %get-tuple-element.36) | copy-start | bytes 772
  22.0 57.7 %all-to-all-start.2 = ((bf16[64,12,512]{2,1,0:T(8,128)(2,1)}), bf16[64,12,512]{2,1,0:T(8,128)(2,1)}, u32[]{:S(2)}, u32[]{:S(2)}) async-start(bf16[64,12,512]{2,1,0:T(8,128)(2,1)} %bitcast.86), calls=%async_computation.2 | async-start | bytes 2097152 | tf_op jit(solution)/shard_map/all_to_all | solution.py:114
  47.3 2.3 copy-start.6
  62.7 3.0 copy-start.28
  63.2 4.0 copy-start.9
  63.2 8.9 collective-permute-start.1
  81.8 46.3 %all-to-all-start = ((bf16[64,12,512]{2,1,0:T(8,128)(2,1)}), bf16[64,12,512]{2,1,0:T(8,128)(2,1)}, u32[]{:S(2)}, u32[]{:S(2)}) async-start(bf16[64,12,512]{2,1,0:T(8,128)(2,1)} %bitcast.342), calls=%async_computation | async-start | bytes 2097152 | tf_op jit(solution)/shard_map/all_to_all | solution.py:114
  101.3 4.0 copy-start.10
  101.3 8.6 collective-permute-start.2
  130.3 36.1 %all-to-all-start.4 = ((bf16[64,12,512]{2,1,0:T(8,128)(2,1)}), bf16[64,12,512]{2,1,0:T(8,128)(2,1)}, u32[]{:S(2)}, u32[]{:S(2)}) async-start(bf16[64,12,512]{2,1,0:T(8,128)(2,1)} %bitcast.340), calls=%async_computation.4 | async-start | bytes 2097152 | tf_op jit(solution)/shard_map/all_to_all | solution.py:114
  146.1 3.6 copy-start.31
  147.3 30.0 %collective-permute-start.3 = (bf16[32,3072]{1,0:T(8,128)(2,1)}, bf16[32,3072]{1,0:T(8,128)(2,1)}, u32[]{:S(2)}, u32[]{:S(2)}) collective-permute-start(bf16[32,3072]{1,0:T(8,128)(2,1)} %fusion.3), channel_id=1, source_target_pairs={{128,0},{256,128},{384,256},{129,1},{257,129},{385,257},{130,2},{2... | collective-permute-start | bytes 589832 | tf_op jit(solution)/shard_map/ppermute | solution.py:12
  168.6 35.7 %all-to-all-start.6 = ((bf16[64,12,512]{2,1,0:T(8,128)(2,1)}), bf16[64,12,512]{2,1,0:T(8,128)(2,1)}, u32[]{:S(2)}, u32[]{:S(2)}) async-start(bf16[64,12,512]{2,1,0:T(8,128)(2,1)} %bitcast.341), calls=%async_computation.6 | async-start | bytes 2097152 | tf_op jit(solution)/shard_map/all_to_all | solution.py:114
  207.4 11.9 %copy-start.20 = (f32[32,2]{0,1:T(2,128)S(1)}, f32[32,2]{0,1:T(2,128)}, u32[]{:S(2)}) copy-start(f32[32,2]{0,1:T(2,128)} %get-tuple-element.36) | copy-start | bytes 772
  207.4 89.4 %all-to-all-start.1 = ((bf16[64,12,1536]{2,1,0:T(8,128)(2,1)}), bf16[64,12,1536]{2,1,0:T(8,128)(2,1)}, u32[]{:S(2)}, u32[]{:S(2)}) async-start(bf16[64,12,1536]{2,1,0:T(8,128)(2,1)} %bitcast.336), calls=%async_computation.1 | async-start | bytes 6291456 | tf_op jit(solution)/shard_map/all_to_all | solution.py:115
  216.2 6.8 copy-start.15
  216.2 6.8 copy-start.17
  220.5 9.2 %collective-permute-start.4 = (bf16[32,3072]{1,0:T(8,128)(2,1)}, bf16[32,3072]{1,0:T(8,128)(2,1)}, u32[]{:S(2)}, u32[]{:S(2)}) collective-permute-start(bf16[32,3072]{1,0:T(8,128)(2,1)} %fusion.4), channel_id=1, source_target_pairs={{128,0},{256,128},{384,256},{129,1},{257,129},{385,257},{130,2},{2... | collective-permute-start | bytes 589832 | tf_op jit(solution)/shard_map/ppermute | solution.py:12
  299.9 99.7 %all-to-all-start.3 = ((bf16[64,12,1536]{2,1,0:T(8,128)(2,1)}), bf16[64,12,1536]{2,1,0:T(8,128)(2,1)}, u32[]{:S(2)}, u32[]{:S(2)}) async-start(bf16[64,12,1536]{2,1,0:T(8,128)(2,1)} %bitcast.338), calls=%async_computation.3 | async-start | bytes 6291456 | tf_op jit(solution)/shard_map/all_to_all | solution.py:115
  323.1 6.8 copy-start.18
  327.5 9.1 %collective-permute-start.5 = (bf16[32,3072]{1,0:T(8,128)(2,1)}, bf16[32,3072]{1,0:T(8,128)(2,1)S(1)}, u32[]{:S(2)}, u32[]{:S(2)}) collective-permute-start(bf16[32,3072]{1,0:T(8,128)(2,1)} %fusion.5), channel_id=1, source_target_pairs={{128,0},{256,128},{384,256},{129,1},{257,129},{385,257},{130,2},{2... | collective-permute-start | bytes 589832 | tf_op jit(solution)/shard_map/ppermute | solution.py:12
  337.2 0.8 copy-start.4
  401.7 25.8 %copy-start.8 = (bf16[32,3072]{1,0:T(8,128)(2,1)S(1)}, bf16[32,3072]{1,0:T(8,128)(2,1)}, u32[]{:S(2)}) copy-start(bf16[32,3072]{1,0:T(8,128)(2,1)} %copy-done.7) | copy-start | bytes 589828
  401.7 25.9 %copy-start.3 = (bf16[1,4,32,1536]{3,2,1,0:T(8,128)(2,1)S(1)}, bf16[1,4,32,1536]{3,2,1,0:T(8,128)(2,1)}, u32[]{:S(2)}) copy-start(bf16[1,4,32,1536]{3,2,1,0:T(8,128)(2,1)} %param.7) | copy-start | bytes 1179652
  401.7 25.9 %copy-start.29 = (f32[32]{0:T(128)S(1)}, f32[32]{0:T(128)}, u32[]{:S(2)}) copy-start(f32[32]{0:T(128)} %copy-done.28) | copy-start | bytes 388
  401.7 27.0 %copy-start.30 = (f32[32]{0:T(128)S(1)}, f32[32]{0:T(128)}, u32[]{:S(2)}) copy-start(f32[32]{0:T(128)} %fusion.177) | copy-start | bytes 388
  401.7 28.1 %copy-start.32 = (f32[32]{0:T(128)S(1)}, f32[32]{0:T(128)}, u32[]{:S(2)}) copy-start(f32[32]{0:T(128)} %copy-done.31) | copy-start | bytes 388
  401.7 98.6 %all-to-all-start.5 = ((bf16[64,12,1536]{2,1,0:T(8,128)(2,1)}), bf16[64,12,1536]{2,1,0:T(8,128)(2,1)}, u32[]{:S(2)}, u32[]{:S(2)}) async-start(bf16[64,12,1536]{2,1,0:T(8,128)(2,1)} %bitcast.337), calls=%async_computation.5 | async-start | bytes 6291456 | tf_op jit(solution)/shard_map/all_to_all | solution.py:115
  502.4 24.2 %copy-start.11 = (bf16[32,3072]{1,0:T(8,128)(2,1)S(1)}, bf16[32,3072]{1,0:T(8,128)(2,1)}, u32[]{:S(2)}) copy-start(bf16[32,3072]{1,0:T(8,128)(2,1)} %get-tuple-element.18) | copy-start | bytes 589828
  502.4 387.6 %all-to-all-start.7 = ((bf16[64,12,1536]{2,1,0:T(8,128)(2,1)}), bf16[64,12,1536]{2,1,0:T(8,128)(2,1)}, u32[]{:S(2)}, u32[]{:S(2)}) async-start(bf16[64,12,1536]{2,1,0:T(8,128)(2,1)} %bitcast.335), calls=%async_computation.7 | async-start | bytes 6291456 | tf_op jit(solution)/shard_map/all_to_all | solution.py:115
  524.3 5.6 copy-start.27
  524.4 345.6 %copy-start.5 = (f32[32,3072]{1,0:T(8,128)S(1)}, f32[32,3072]{1,0:T(8,128)}, u32[]{:S(2)}) copy-start(f32[32,3072]{1,0:T(8,128)} %copy-done.4) | copy-start | bytes 1179652
  870.1 6.1 copy-start.12
where the time goes:
time: 910 us; the launch traced here: 899 us
  blocking collectives  362 us (40%)
  waiting for transfers between devices  257 us (28%)
  starting transfers between devices  145 us (16%)
  local copies, waits for them, and re-layouts  57 us (6%)
  matrix products  48.4 us (5%)
  other arithmetic  26.8 us (3%)
    unnamed x1, blocking collectives  339 us
    all_to_all x4, waiting for transfers between devices, per_device(): lax.all_to_all(scaled_slots, 'ed', split_axis=0, concat_axis=0, tiled=True)  185 us
    all_to_all x4, starting transfers between devices, per_device(): lax.all_to_all(scaled_slots, 'ed', split_axis=0, concat_axis=0, tiled=True)  77.8 us
    all_to_all x4, starting transfers between devices, per_device(): lax.all_to_all(hidden_slots, 'ed', split_axis=0, concat_axis=0, tiled=True)  52.8 us
    all_to_all x4, waiting for transfers between devices, per_device(): lax.all_to_all(hidden_slots, 'ed', split_axis=0, concat_axis=0, tiled=True)  49.6 us
    dot_general x4, matrix products, per_device(): jnp.einsum('scf,scd->fd', got_hidden, got_scaled, preferred_element_type=...  28.1 us
    ppermute x6, waiting for transfers between devices, from_behind(): return lax.ppermute(shard, axis, pairs)  22.6 us
    psum x7, blocking collectives, per_device(): gate_grad = lax.psum(partial_dots, 'tp')  20.2 us
  transfers between devices with their start and end apart: 14, of which 10 were waited for; matrix products, arithmetic and copies ran while one was open for 12% of the time, Pallas kernels for 0%

commit v1 on v0

v1 whole, which is shorter than its diff:
```python
import jax
import jax.numpy as jnp
from jax import lax
from jax.experimental import pallas as pl
from jax.experimental.pallas import tpu as pltpu
from jax.sharding import PartitionSpec as P

CAP = 12
MICRO = 4
TOK = 32
SIDE = 8
SECTIONS = 4
EXPERTS = 8
WINDOW = 4
HIGHEST = lax.Precision.HIGHEST
F32 = jnp.float32
BF16 = jnp.bfloat16
MESH = pl.DeviceIdType.MESH


def iota(shape, dim):
    return lax.broadcasted_iota(jnp.int32, shape, dim)


def divided(x, by):
    return ((x.astype(F32) + 0.5) * (1.0 / by)).astype(jnp.int32)


def contract(a, b, da, db, precision=None):
    return lax.dot_general(a, b, (((da,), (db,)), ((), ())), precision=precision, preferred_element_type=F32)


def split2(x):
    hi = x.astype(BF16)
    return hi, (x - hi.astype(F32)).astype(BF16)


def split3(x):
    hi = x.astype(BF16)
    rest = x - hi.astype(F32)
    mid = rest.astype(BF16)
    return hi, mid, (rest - mid.astype(F32)).astype(BF16)


def by_parts(x, rows, dims):
    parts = jnp.concatenate([p.astype(F32) for p in split3(x)], axis=0).astype(BF16)
    got = contract(parts, rows, 1, dims)
    n = x.shape[0]
    return got[:n] + got[n:2 * n] + got[2 * n:]


def earlier(segment_log2):
    r, c = iota((256, 256), 0), iota((256, 256), 1)
    same = jnp.right_shift(r, segment_log2) == jnp.right_shift(c, segment_log2)
    return jnp.where(same & (r < c), 1.0, 0.0).astype(BF16)


def kernel(
    top_ref, x_ref, w_ref, idr_ref, idt_ref, eo_ref, hid_ref,
    cot_ref, down_ref, router_ref,
    wb, pr, sm, szr, sg, ry, ryr, rz, rzr, topb, pick, hs, hy, hz, perm, seg, wq, xs, rel, sc, acc,
    w_s, w_r, p_s, p_r, tz_s, tz_r, ring_s, ring_r, sz_s, sz_r, sy_s, sy_r, ry_s, ry_r, rz_s, rz_r,
    hy_s, hy_r, hz_s, hz_r, hf_s, xx_s, xx_r, rr_s, rr_r, cc_s, cc_r,
):
    x = lax.axis_index("section")
    ed = lax.axis_index("ed")
    c = lax.axis_index("tp")
    y = ed // SIDE
    z = ed % SIDE
    half = top_ref.shape[2]
    quarter = half // 2
    own_half = z % 2
    own_expert = y // 2

    def at_x(k):
        return ((x + k) % SECTIONS, ed, c)

    def at_y(k):
        return (x, ((y + k) % SIDE) * SIDE + z, c)

    def at_z(k):
        return (x, y * SIDE + (z + k) % SIDE, c)

    partner = (x, ed, 1 - c)

    def off(i):
        return ((i + 1) // 2) * (1 - 2 * (i % 2))

    def source(i):
        return (y + SIDE + off(i)) % SIDE

    def copy(src, dst, send, recv, device):
        return pltpu.make_async_remote_copy(
            src_ref=src, dst_ref=dst, send_sem=send, recv_sem=recv, device_id=device, device_id_type=MESH
        )

    barrier = pltpu.get_barrier_semaphore()

    def greet(device):
        pl.semaphore_signal(barrier, inc=1, device_id=device, device_id_type=MESH)

    greet(partner)
    for k in range(1, SECTIONS):
        for cc in range(2):
            greet(((x + k) % SECTIONS, ed, cc))
    for k in range(1, SIDE):
        greet(at_y(k))
        for cc in range(2):
            greet((x, y * SIDE + (z + k) % SIDE, cc))

    ids_row = idr_ref[...]
    named = (jnp.broadcast_to(ids_row, (8, 256)) == iota((8, 256), 0)).astype(F32)
    rank = jnp.dot(named.astype(BF16), earlier(6), preferred_element_type=F32)
    r48 = iota((48, 256), 0)
    m48 = divided(r48, CAP)
    s48 = (r48 - CAP * m48).astype(F32)
    own_micro = m48 == jnp.right_shift(iota((48, 256), 1), 6)
    for e in range(WINDOW):
        hit = (
            (jnp.broadcast_to(named[e:e + 1], (48, 256)) > 0.5)
            & (jnp.broadcast_to(rank[e:e + 1], (48, 256)) == s48)
            & own_micro
        )
        pick[e * 48:(e + 1) * 48, :] = jnp.where(hit, 1.0, 0.0).astype(BF16)

    pl.semaphore_wait(barrier, 1 + 2 * (SECTIONS - 1) + 3 * (SIDE - 1))

    def w_copy(k):
        return copy(w_ref, wb.at[x], w_s.at[k - 1], w_r.at[k - 1], at_x(k))

    for k in range(1, SECTIONS):
        w_copy(k).start()
    wb[x] = w_ref[...]

    tilt = (z + c) % 2
    local = tilt == 0

    def tz_copy(r, cc):
        zd = (z + 2 * r + tilt) % SIDE
        return copy(
            top_ref.at[x, :, pl.ds(cc * quarter, quarter)], topb.at[y, z], tz_s.at[r, cc], tz_r.at[z],
            (x, y * SIDE + zd, cc),
        )

    for r in range(4):
        for cc in range(2):
            if r == 0:
                @pl.when(jnp.logical_not(local & (c == cc)))
                def _():
                    tz_copy(r, cc).start()
            else:
                tz_copy(r, cc).start()

    @pl.when(local)
    def _():
        topb[y, z] = top_ref[x, :, pl.ds(pl.multiple_of(c * quarter, 128), quarter)]

    def hidden_block(f, carry):
        cols = hid_ref[:, pl.ds(pl.multiple_of(f * 512, 512), 512)]
        got = jnp.dot(pick[...], cols, preferred_element_type=F32).astype(BF16)
        for e in range(WINDOW):
            hs[2 * e + f // 4, f % 4] = got[e * 48:(e + 1) * 48]
        return carry

    lax.fori_loop(0, 8, hidden_block, 0)

    def hy_copy(i):
        yd = (y + SIDE - off(i)) % SIDE
        return copy(hs.at[yd], hy.at[y], hy_s.at[0], hy_r.at[i], (x, yd * SIDE + z, c))

    def hy_start(i, carry):
        hy_copy(i).start()
        return carry

    def ring_copy(block, first, count, item, k):
        part = topb.at[block, pl.ds(first, count)]
        return copy(part, part, ring_s.at[0], ring_r.at[item], at_y(k))

    def tz_wait(zs, carry):
        @pl.when(jnp.logical_not(local & (zs == z)))
        def _():
            copy(topb.at[y, zs], topb.at[y, zs], tz_s.at[0, 0], tz_r.at[zs], partner).wait_recv()
        return carry

    lax.fori_loop(0, SIDE, tz_wait, 0)
    ring_copy(y, 0, SIDE, 1, 1).start()
    ring_copy(y, 0, SIDE, 2, SIDE - 1).start()
    lax.fori_loop(1, 5, hy_start, 0)
    hy[y] = hs[y]

    pair = z // 2
    parity = z % 2

    def hz_copy(i, d):
        ys = source(i)
        if d == 0:
            target, j = z + 1 - 2 * parity, 1
        elif d == 1:
            target, j = 2 * ((pair + 1) % 4), 0
        elif d == 2:
            target, j = 2 * ((pair + 2) % 4) + 1 - parity, 0
        else:
            target, j = 2 * ((pair + 3) % 4) + 1, 0
        return copy(
            hy.at[ys, (pair + d) % 4], hz.at[z, ys], hz_s.at[0], hz_r.at[i, j], (x, y * SIDE + target, c)
        )

    def send_hidden(i):
        ys = source(i)
        for d in (2, 1, 3, 0):
            hz_copy(i, d).start()
        hz[z, ys] = hy[ys, pair]

    near = 2 * ((pair + 3 + 2 * parity) % 4)
    far = 2 * ((pair + 2) % 4) + 1 - parity
    other = (x, y * SIDE + z + 1 - 2 * parity, c)

    def forward_hidden(i):
        ys = source(i)
        three = hz.at[pl.ds(0, 3), ys]
        copy(three, three, hz_s.at[0], hz_r.at[i, 0], partner).wait_recv()
        two, one = hz.at[pl.ds(near, 2), ys], hz.at[far, ys]
        copy(two, two, hf_s.at[0], hz_r.at[i, 1], other).start()
        copy(one, one, hf_s.at[0], hz_r.at[i, 1], other).start()

    def wait_hidden(i):
        four = hz.at[pl.ds(0, 4), source(i)]
        copy(four, four, hz_s.at[0], hz_r.at[i, 1], partner).wait_recv()

    send_hidden(0)

    core_cols = pl.ds(pl.multiple_of(c * half, 128), half)
    inputs = x_ref[...]
    top_tokens = top_ref[...].reshape(MICRO * TOK, half)
    outs = eo_ref[...]
    r128, c256 = iota((128, 256), 0), iota((128, 256), 1)
    pairs = jnp.where(c256 == 2 * r128, 1.0, jnp.where(c256 == 2 * r128 + 1, -1.0, 0.0))
    pr[x, c, 0:8] = by_parts(w_ref[:, core_cols], inputs, 1)
    products = contract(top_tokens, outs, 1, 1)
    dots = jnp.sum(products * jnp.abs(pairs), axis=0, keepdims=True)
    pr[x, c, 8:16] = contract(jnp.broadcast_to(dots, (8, 256)), pairs, 1, 1, HIGHEST)
    pr[x, c, 9:11] = idt_ref[...]

    def w_wait(k):
        copy(w_ref, wb.at[(x + SECTIONS - k) % SECTIONS], w_s.at[k - 1], w_r.at[k - 1], at_x(k)).wait_recv()

    for k in range(1, SECTIONS):
        w_wait(k)
    weights_half = wb[:, :, core_cols]
    crossed = by_parts(weights_half.reshape(SECTIONS * EXPERTS, half), outs, 1)
    pr[x, c, 16:48] = contract(crossed, pairs, 1, 1, HIGHEST)

    def p_copy(n):
        dx, dc = n // 2, n % 2
        return copy(pr.at[x, c], pr.at[x, c], p_s.at[n - 1], p_r.at[n - 1], ((x + dx) % SECTIONS, ed, (c + dc) % 2))

    for n in range(1, 2 * SECTIONS):
        p_copy(n).start()

    seg[...] = earlier(5)
    rp, cp = iota((384, 384), 0), iota((384, 384), 1)
    qp = divided(rp, CAP)
    perm[...] = jnp.where(
        cp == (qp & 7) * 48 + jnp.right_shift(qp, 3) * CAP + rp - CAP * qp, 1.0, 0.0
    ).astype(BF16)
    w_quarter = wb[:, :, pl.ds(pl.multiple_of(own_half * half + c * quarter, 128), quarter)]
    w_hi, w_mid = split2(w_quarter.reshape(SECTIONS * EXPERTS, quarter))
    wq[0:32] = w_hi
    wq[32:64] = w_hi
    wq[64:96] = w_mid
    wq[96:128] = jnp.zeros((32, quarter), BF16)
    ry[...] = jnp.zeros_like(ry)
    rz[...] = jnp.zeros_like(rz)

    for n in range(1, 2 * SECTIONS):
        dx, dc = n // 2, n % 2
        part = pr.at[(x + SECTIONS - dx) % SECTIONS, (c + dc) % 2]
        copy(part, part, p_s.at[n - 1], p_r.at[n - 1], partner).wait_recv()

    j8 = iota((8, 128), 0).astype(F32)
    firsts, grads, selects, dls = [], [None] * SECTIONS, [], [None] * SECTIONS
    for l in range(SECTIONS):
        logits = pr[l, 0, 0:8] + pr[l, 1, 0:8]
        id0, id1 = pr[l, 0, 9:10], pr[l, 0, 10:11]
        hot0 = jnp.where(jnp.broadcast_to(id0, (8, 128)) == j8, 1.0, 0.0)
        hot1 = jnp.where(jnp.broadcast_to(id1, (8, 128)) == j8, 1.0, 0.0)
        selects.append(hot0 - hot1)
        gap = jnp.sum(hot1 * logits, axis=0, keepdims=True) - jnp.sum(hot0 * logits, axis=0, keepdims=True)
        firsts.append(1.0 / (1.0 + jnp.exp(gap)))
        sm[4 + l:5 + l] = firsts[l]
        sm[8 + l:9 + l] = id0
        sm[12 + l:13 + l] = id1
    for l in range(SECTIONS - 1, -1, -1):
        total = pr[l, 0, 8:9] + pr[l, 1, 8:9]
        for a in range(l + 1, SECTIONS):
            cross = pr[l, 0, 16 + 8 * a:24 + 8 * a] + pr[l, 1, 16 + 8 * a:24 + 8 * a]
            total = total + grads[a] * jnp.sum(cross * selects[a], axis=0, keepdims=True)
        grads[l] = firsts[l] * (1.0 - firsts[l]) * total
        sm[l:l + 1] = grads[l]
        dls[l] = jnp.broadcast_to(grads[l], (8, 128)) * selects[l]

    to = iota((128, 256), 1) - z * TOK
    at = iota((128, 256), 0) - x * TOK
    put = jnp.where((to == at) & (to >= 0) & (to < TOK), 1.0, 0.0)
    szr[z] = jnp.dot(sm[...], put, precision=HIGHEST, preferred_element_type=F32)

    def sz_copy(k):
        return copy(szr.at[z], szr.at[z], sz_s.at[k - 1], sz_r.at[k - 1], at_z(k))

    for k in range(1, SIDE):
        sz_copy(k).start()

    def take_ring(i):
        part = topb.at[source(i)]
        copy(part, part, ring_s.at[0], ring_r.at[i], partner).wait_recv()

        @pl.when(i < 5)
        def _():
            ring_copy(source(i), 0, SIDE, i + 2, 1 + (1 - i % 2) * (SIDE - 2)).start()

        @pl.when(i == 5)
        def _():
            ring_copy(source(i), 0, 4, SIDE - 1, 1).start()

        @pl.when(i == 6)
        def _():
            ring_copy(source(i), 4, 4, SIDE - 1, SIDE - 1).start()

        @pl.when((i >= 2) & (i < 5))
        def _():
            hy_copy(i + 3).start()

    own_dl = jnp.zeros((8, 128), F32)
    for l in range(SECTIONS):
        own_dl = jnp.where(x == l, dls[l], own_dl)
    router_part = by_parts(own_dl, inputs, 0)
    strip = half // SIDE
    for k in range(SIDE):
        ry[k, :, 0:strip] = router_part[:, k * strip:(k + 1) * strip]

    def ry_copy(k):
        yd = (y + k) % SIDE
        return copy(ry.at[yd], ryr.at[y], ry_s.at[k - 1], ry_r.at[k - 1], at_y(k))

    for k in range(1, SIDE):
        ry_copy(k).start()
    ryr[y] = ry[y]

    def first_rings(i, carry):
        take_ring(i)
        return carry

    lax.fori_loop(1, 3, first_rings, 0)

    for k in range(1, SIDE):
        part = szr.at[(z + SIDE - k) % SIDE]
        copy(part, part, sz_s.at[k - 1], sz_r.at[k - 1], partner).wait_recv()
    total = szr[0]
    for k in range(1, SIDE):
        total = total + szr[k]
    sg[y] = total

    def sy_copy(i):
        return copy(sg.at[y], sg.at[y], sy_s.at[i], sy_r.at[i], at_y(SIDE - off(i)))

    for i in range(1, SIDE):
        sy_copy(i).start()

    def rz_copy(k):
        zd = (z + k) % SIDE
        return copy(rz.at[zd], rzr.at[z], rz_s.at[k - 1], rz_r.at[k - 1], at_z(k))

    def router_second():
        for k in range(1, SIDE):
            part = ryr.at[(y + SIDE - k) % SIDE]
            copy(part, part, ry_s.at[k - 1], ry_r.at[k - 1], partner).wait_recv()
        total = ryr[0]
        for k in range(1, SIDE):
            total = total + ryr[k]
        piece = strip // SIDE
        for k in range(SIDE):
            rz[k, :, 0:piece] = total[:, k * piece:(k + 1) * piece]
        for k in range(1, SIDE):
            rz_copy(k).start()
        rzr[z] = rz[z]

    def cotangents():
        cotangent = top_tokens
        for l in range(SECTIONS - 1, -1, -1):
            d_hi, d_mid, _ = split3(dls[l])
            w_hi, w_mid, _ = split3(wb[l, :, core_cols])
            left = jnp.concatenate([d.astype(F32) for d in (d_hi, d_mid, d_hi)], axis=0).astype(BF16)
            right = jnp.concatenate([w.astype(F32) for w in (w_hi, w_hi, w_mid)], axis=0).astype(BF16)
            step = contract(left, right, 0, 0)
            cotangent = jnp.where(l >= x, (cotangent.astype(F32) + step).astype(BF16), cotangent)
        cot_ref[...] = cotangent

    def take_hidden(i):
        copy(hs.at[0], hy.at[source(i)], hy_s.at[0], hy_r.at[i], partner).wait_recv()
        send_hidden(i)

    def x_copy(i, n):
        ys = source(i)
        if n < 2:
            k = 1 + 2 * n
            return copy(
                xs.at[i, (x + k) % SECTIONS], sc.at[c, ys, x], xx_s.at[0], xx_r.at[i], at_x(k)
            )
        n -= 2
        return copy(
            xs.at[i, (x + 2) % SECTIONS, pl.ds(48 * n, 48)], rel.at[i, n], xx_s.at[0], rr_r.at[i, n],
            at_x(1 + 2 * n),
        )

    def relay_copy(i, n):
        k = 1 + 2 * n
        return copy(
            rel.at[i, n], sc.at[c, source(i), (x + SECTIONS - k) % SECTIONS, pl.ds(48 * n, 48)],
            rr_s.at[0], xx_r.at[i], at_x(k),
        )

    def relay(i):
        for n in range(2):
            copy(rel.at[i, n], rel.at[i, n], rr_s.at[0], rr_r.at[i, n], partner).wait_recv()
            relay_copy(i, n).start()

    def core_copy(i):
        part = sc.at[c, source(i)]
        return copy(part, part, cc_s.at[0], cc_r.at[i], partner)

    r96 = iota((96, 256), 0)
    z96 = divided(r96, CAP)
    s96 = (r96 - CAP * z96).astype(F32)
    own_block = z96 == jnp.right_shift(iota((96, 256), 1), 5)
    mine = own_expert.astype(F32)

    def select(i):
        ys = source(i)
        small = sg[ys]
        grad, first, id0, id1 = small[0:4], small[4:8], small[8:12], small[12:16]
        is0, is1 = id0 == mine, id1 == mine
        named = jnp.where(is0 | is1, 1.0, 0.0)
        gate = jnp.where(is0, first, 1.0 - first)
        rank = jnp.dot(
            jnp.concatenate([named, named], axis=0).astype(BF16), seg[...], preferred_element_type=F32
        )
        dl = []
        jt = iota((8, 256), 0).astype(F32)
        for l in range(SECTIONS):
            sel = jnp.where(jnp.broadcast_to(id0[l:l + 1], (8, 256)) == jt, 1.0, 0.0)
            sel = sel - jnp.where(jnp.broadcast_to(id1[l:l + 1], (8, 256)) == jt, 1.0, 0.0)
            dl.append(jnp.broadcast_to(grad[l:l + 1], (8, 256)) * sel)
        d_hi, d_mid = split2(jnp.concatenate(dl, axis=0))
        side = jnp.concatenate([d_hi, d_mid, d_hi, jnp.zeros_like(d_hi)], axis=0)
        tops = topb[ys].reshape(SIDE * TOK, quarter)
        places, gates = [], []
        for l in range(SECTIONS):
            hit = (
                (jnp.broadcast_to(named[l:l + 1], (96, 256)) > 0.5)
                & (jnp.broadcast_to(rank[l:l + 1], (96, 256)) == s96)
                & own_block
            )
            gates.append(jnp.sum(
                jnp.where(hit, jnp.broadcast_to(gate[l:l + 1], (96, 256)), 0.0), axis=1, keepdims=True
            ))
            places.append(jnp.where(hit, 1.0, 0.0).astype(BF16))
        place = jnp.concatenate(places, axis=0)
        lefts = contract(place, side, 1, 1)
        above = jnp.right_shift(iota((96, 128), 1) & 31, 3)
        left = jnp.concatenate(
            [jnp.where(above > l, lefts[96 * l:96 * (l + 1)], 0.0).astype(BF16) for l in range(SECTIONS)], axis=0
        )
        rows = jnp.dot(place, tops, preferred_element_type=F32)
        rows = rows + jnp.dot(left, wq[...], preferred_element_type=F32)
        for l in range(SECTIONS):
            xs[i, l] = (gates[l] * rows[96 * l:96 * (l + 1)]).astype(BF16)
        for n in (2, 3, 0, 1):
            x_copy(i, n).start()
        sc[c, ys, x] = xs[i, x]

    def to_partner(i):
        three = sc.at[c, source(i), pl.ds(0, 3)]
        copy(three, three, xx_s.at[0], xx_r.at[i], partner).wait_recv()
        core_copy(i).start()

    def accumulate(i):
        ys = source(i)
        wait_hidden(i)
        part = sc.at[1 - c, ys]
        copy(part, part, cc_s.at[0], cc_r.at[i], partner).wait_recv()
        rows = jnp.dot(perm[...], hz[:, ys].reshape(384, 512), preferred_element_type=F32).astype(BF16)
        for q in range(2):
            cols = slice(q * quarter, (q + 1) * quarter)
            acc[:, cols] += contract(rows, sc[q, ys].reshape(384, quarter), 0, 0)

    acc[...] = jnp.zeros_like(acc)

    def small_wait(i):
        copy(sg.at[source(i)], sg.at[source(i)], sy_s.at[i], sy_r.at[i], partner).wait_recv()

    def body(i, carry):
        @pl.when((i >= 1) & (i < SIDE - 2))
        def _():
            take_ring(i + 2)

        @pl.when(i < SIDE - 1)
        def _():
            take_hidden(i + 1)

        @pl.when((i >= 1) & (i < SIDE))
        def _():
            small_wait(i)

        @pl.when(i < SIDE)
        def _():
            select(i)

        @pl.when((i >= 1) & (i < SIDE + 1))
        def _():
            forward_hidden(i - 1)
            relay(i - 1)

        @pl.when((i >= 2) & (i < SIDE + 2))
        def _():
            to_partner(i - 2)

        @pl.when(i == 2)
        def _():
            router_second()

        @pl.when(i == 1)
        def _():
            cotangents()

        @pl.when(i >= 3)
        def _():
            accumulate(i - 3)

        return carry

    lax.fori_loop(0, SIDE + 3, body, 0)
    down_ref[...] = acc[...].astype(BF16)
    for k in range(1, SIDE):
        part = rzr.at[(z + SIDE - k) % SIDE]
        copy(part, part, rz_s.at[k - 1], rz_r.at[k - 1], partner).wait_recv()
    total = rzr[0]
    for k in range(1, SIDE):
        total = total + rzr[k]
    router_ref[...] = total

    for k in range(1, SECTIONS):
        w_copy(k).wait_send()
    for n in range(1, 2 * SECTIONS):
        p_copy(n).wait_send()
    for r in range(4):
        for cc in range(2):
            if r == 0:
                @pl.when(jnp.logical_not(local & (c == cc)))
                def _():
                    tz_copy(r, cc).wait_send()
            else:
                tz_copy(r, cc).wait_send()
    for k in range(1, SIDE):
        sz_copy(k).wait_send()
        sy_copy(k).wait_send()
        ry_copy(k).wait_send()
        rz_copy(k).wait_send()


    def drained(ref, sem):
        copy(ref, ref, sem.at[0], cc_r.at[0], partner).wait_send()

    drained(topb.at[pl.ds(0, SIDE - 1)], ring_s)
    drained(hy.at[pl.ds(0, SIDE - 1)], hy_s)
    drained(hy, hz_s)
    drained(hy.at[:, pl.ds(0, 3)], hf_s)
    drained(xs.at[:, pl.ds(0, 3)], xx_s)
    drained(rel, rr_s)
    drained(xs, cc_s)


def per_device(top_cotangent, layer_inputs, router_weight, expert_ids, expert_outputs, hidden):
    micro, tok, half = top_cotangent.shape
    tokens = micro * tok
    half_ff = hidden.shape[4]
    width = router_weight.shape[1]
    quarter = half // 2
    tile = half_ff // SIDE
    strip = half // SIDE // SIDE
    vmem = pl.BlockSpec(memory_space=pltpu.VMEM)
    dma = pltpu.SemaphoreType.DMA
    hidden_rows = MICRO * CAP
    scratch = [
        pltpu.VMEM((SECTIONS, EXPERTS, width), F32),
        pltpu.VMEM((SECTIONS, 2, 48, tokens), F32),
        pltpu.VMEM((16, tokens), F32),
        pltpu.VMEM((SIDE, 16, SIDE * TOK), F32),
        pltpu.VMEM((SIDE, 16, SIDE * TOK), F32),
        pltpu.VMEM((SIDE, EXPERTS, 256), F32),
        pltpu.VMEM((SIDE, EXPERTS, 256), F32),
        pltpu.VMEM((SIDE, EXPERTS, 128), F32),
        pltpu.VMEM((SIDE, EXPERTS, 128), F32),
        pltpu.VMEM((SIDE, SIDE, TOK, quarter), BF16),
        pltpu.VMEM((WINDOW * hidden_rows, 256), BF16),
        pltpu.VMEM((SIDE, 4, hidden_rows, tile), BF16),
        pltpu.VMEM((SIDE, 4, hidden_rows, tile), BF16),
        pltpu.VMEM((SIDE, SIDE, hidden_rows, tile), BF16),
        pltpu.VMEM((384, 384), BF16),
        pltpu.VMEM((256, 256), BF16),
        pltpu.VMEM((128, quarter), BF16),
        pltpu.VMEM((SIDE, SECTIONS, SIDE * CAP, quarter), BF16),
        pltpu.VMEM((SIDE, 2, SIDE * CAP // 2, quarter), BF16),
        pltpu.VMEM((2, SIDE, SECTIONS, SIDE * CAP, quarter), BF16),
        pltpu.VMEM((tile, half), F32),
        dma((3,)), dma((3,)),
        dma((7,)), dma((7,)),
        dma((4, 2)), dma((SIDE,)),
        dma((1,)), dma((SIDE,)),
        dma((7,)), dma((7,)),
        dma((SIDE,)), dma((SIDE,)),
        dma((7,)), dma((7,)),
        dma((7,)), dma((7,)),
        dma((1,)), dma((SIDE,)),
        dma((1,)), dma((SIDE, 2)),
        dma((1,)),
        dma((1,)), dma((SIDE,)),
        dma((1,)), dma((SIDE, 2)),
        dma((1,)), dma((SIDE,)),
    ]
    cotangent, down, router = pl.pallas_call(
        kernel,
        out_shape=(
            jax.ShapeDtypeStruct((tokens, half), BF16),
            jax.ShapeDtypeStruct((tile, half), BF16),
            jax.ShapeDtypeStruct((EXPERTS, 128), F32),
        ),
        in_specs=[vmem] * 7,
        out_specs=(vmem, vmem, vmem),
        scratch_shapes=scratch,
        compiler_params=pltpu.CompilerParams(
            collective_id=0, has_side_effects=True, vmem_limit_bytes=50 * 1024 * 1024
        ),
        cost_estimate=pl.CostEstimate(flops=8_000_000_000, bytes_accessed=8_000_000, transcendentals=0),
    )(
        top_cotangent,
        layer_inputs.reshape(tokens, half),
        router_weight[0].T,
        expert_ids.reshape(1, tokens * 2),
        expert_ids.reshape(tokens, 2).T.astype(F32),
        expert_outputs.reshape(tokens * 2, half),
        hidden.reshape(tokens * 2, half_ff),
    )
    return (
        cotangent.reshape(1, micro, tok, half),
        down.reshape(1, 1, 1, tile, half),
        router[:, :strip].T.reshape(1, 1, strip, EXPERTS),
    )


def solution(mesh):
    in_specs = (
        P(None, "ed", "tp"),
        P("section", None, "ed", "tp"),
        P("section", None, None),
        P("section", None, "ed", None),
        P("section", None, "ed", None, "tp"),
        P("section", None, "ed", None, "tp"),
    )
    out_specs = (
        P("section", None, "ed", "tp"),
        P("section", "tp", "ed", None, None),
        P("section", "tp", "ed", None),
    )
    return jax.shard_map(
        per_device, mesh=mesh, in_specs=in_specs, out_specs=out_specs, check_vma=False
    )
```

time: 910 us -> 140 us (0.15)
  the two profiles are of different devices: /device:TPU:36 before, /device:TPU:1 now
where the time goes in v1:
time: 140 us; the launch traced here: 139 us
  Pallas kernels  128 us (91%)
  local copies, waits for them, and re-layouts  9.95 us (7%)
    pallas_call x1, Pallas kernels, per_device(): pl.pallas_call(kernel, out_shape=(jax.ShapeDtypeStruct((tokens, half), BF...  128 us
    reshape x1, local copies, waits for them, and re-layouts, per_device(): hidden.reshape(tokens * 2, half_ff)  4.16 us

profile of v1, /device:TPU:1, one launch (start us, length us, event | category | flops | bytes accessed | tf_op | source)
XLA Modules:
  0.0 139.4 jit_solution(1719450479690105325)
XLA Ops:
  0.6 0.7 convert_element_type.7
  1.3 0.1 convert_element_type.8
  1.4 0.8 copy.11
  2.2 0.1 reshape.30.idr_ref
  2.3 2.3 %reshape.31.eo_ref = bf16[256,1536]{1,0:T(8,128)(2,1)S(1)} reshape(bf16[1,4,32,2,1536]{4,3,2,1,0:T(2,128)(2,1)} %param.10) | data formatting | bytes 1572864 | tf_op jit(solution)/shard_map/reshape | solution.py:650
  4.6 0.0 copy-start
  4.6 0.0 copy-start.1
  4.6 0.0 copy-start.2
  4.7 4.2 %reshape.32.hid_ref = bf16[256,4096]{1,0:T(8,128)(2,1)} reshape(bf16[1,4,32,2,4096]{4,3,2,1,0:T(2,128)(2,1)} %param.11) | data formatting | bytes 4194304 | tf_op jit(solution)/shard_map/reshape | solution.py:651
  8.8 0.0 copy-done
  8.8 0.0 copy-done.1
  8.8 0.0 copy-done.2
  8.8 128.1 %shard_map.85 = (bf16[128,1536]{1,0:T(8,128)(2,1)S(1)}, bf16[512,1536]{1,0:T(8,128)(2,1)S(1)}, f32[8,128]{1,0:T(8,128)S(1)}) custom-call(bf16[4,32,1536]{2,1,0:T(8,128)(2,1)S(1)} %copy-done, bf16[128,1536]{1,0:T(8,128)(2,1)S(1)} %bitcast.18, f32[8,3072]{1,0:T(8,128)S(1)} %bitcast.19, s32[1,256]{1,0:T(1,128)S(1)} %reshape.30.idr_ref, f32[2,128]{1,0:T(2,128)S(1)} %bitcast.17, ...), custom_call_target="tpu_custom_call" | custom-call | flops 8000000000 | bytes 8000000 | tf_op jit(solution)/shard_map/pallas_call | solution.py:630
  136.9 0.6 slice_bitcast_fusion
  137.5 0.7 copy.15
  138.3 1.1 copy.16
  (1 shorter events, 0.0 us)
Async XLA Ops:
  4.6 4.2 %copy-start = (bf16[4,32,1536]{2,1,0:T(8,128)(2,1)S(1)}, bf16[4,32,1536]{2,1,0:T(8,128)(2,1)}, u32[]{:S(2)}) copy-start(bf16[4,32,1536]{2,1,0:T(8,128)(2,1)} %top_ref.1) | copy-start | bytes 1179652
  4.6 4.2 %copy-start.1 = (bf16[1,4,32,1536]{3,2,1,0:T(8,128)(2,1)S(1)}, bf16[1,4,32,1536]{3,2,1,0:T(8,128)(2,1)}, u32[]{:S(2)}) copy-start(bf16[1,4,32,1536]{3,2,1,0:T(8,128)(2,1)} %param.7) | copy-start | bytes 1179652
  4.6 4.2 %copy-start.2 = (f32[1,3072,8]{1,2,0:T(8,128)S(1)}, f32[1,3072,8]{1,2,0:T(8,128)}, u32[]{:S(2)}) copy-start(f32[1,3072,8]{1,2,0:T(8,128)} %param.8) | copy-start | bytes 294916

commit v2 on v1

--- a/solution.py
+++ b/solution.py
@@ -185,7 +185,7 @@
     lax.fori_loop(0, SIDE, tz_wait, 0)
     ring_copy(y, 0, SIDE, 1, 1).start()
     ring_copy(y, 0, SIDE, 2, SIDE - 1).start()
-    lax.fori_loop(1, 5, hy_start, 0)
+    lax.fori_loop(1, 3, hy_start, 0)
     hy[y] = hs[y]
 
     pair = z // 2
@@ -326,9 +326,9 @@
         def _():
             ring_copy(source(i), 4, 4, SIDE - 1, SIDE - 1).start()
 
-        @pl.when((i >= 2) & (i < 5))
-        def _():
-            hy_copy(i + 3).start()
+        @pl.when(i < SIDE - 2)
+        def _():
+            hy_copy(i + 2).start()
 
     own_dl = jnp.zeros((8, 128), F32)
     for l in range(SECTIONS):
@@ -499,25 +499,40 @@
         copy(sg.at[source(i)], sg.at[source(i)], sy_s.at[i], sy_r.at[i], partner).wait_recv()
 
     def body(i, carry):
-        @pl.when((i >= 1) & (i < SIDE - 2))
-        def _():
-            take_ring(i + 2)
-
-        @pl.when(i < SIDE - 1)
+        @pl.when(i < 3)
+        def _():
+            forward_hidden(i)
+
+        @pl.when((i >= 4) & (i < SIDE + 1))
+        def _():
+            forward_hidden(i - 1)
+
+        @pl.when((i >= 3) & (i < SIDE) & (i % 2 == 1))
+        def _():
+            take_ring(i)
+
+        @pl.when((i >= 3) & (i < SIDE - 1) & (i % 2 == 1))
+        def _():
+            take_ring(i + 1)
+
+        @pl.when((i >= 1) & (i < SIDE))
+        def _():
+            small_wait(i)
+
+        @pl.when(i < SIDE)
+        def _():
+            select(i)
+
+        @pl.when(i < 2)
         def _():
             take_hidden(i + 1)
 
-        @pl.when((i >= 1) & (i < SIDE))
-        def _():
-            small_wait(i)
-
-        @pl.when(i < SIDE)
-        def _():
-            select(i)
+        @pl.when((i >= 3) & (i < SIDE))
+        def _():
+            take_hidden(i)
 
         @pl.when((i >= 1) & (i < SIDE + 1))
         def _():
-            forward_hidden(i - 1)
             relay(i - 1)
 
         @pl.when((i >= 2) & (i < SIDE + 2))

time: 140 us -> 137 us (0.979)
  Pallas kernels: 128 us -> 126 us
    pallas_call x1, Pallas kernels: 128 us -> 126 us  [per_device(): pl.pallas_call(kernel, out_shape=(jax.ShapeDtypeStruct((tokens, half), BF...]
where the time goes in v2:
time: 137 us
  Pallas kernels  126 us (92%)
  local copies, waits for them, and re-layouts  9.95 us (7%)
    pallas_call x1, Pallas kernels, per_device(): pl.pallas_call(kernel, out_shape=(jax.ShapeDtypeStruct((tokens, half), BF...  126 us
    reshape x1, local copies, waits for them, and re-layouts, per_device(): hidden.reshape(tokens * 2, half_ff)  4.16 us

profile of v2, /device:TPU:1, one launch (start us, length us, event | category | flops | bytes accessed | tf_op | source)
XLA Modules:
  0.0 137.0 jit_solution(8805469740461838545)
XLA Ops:
  0.6 0.7 convert_element_type.7
  1.3 0.1 convert_element_type.8
  1.4 0.8 copy.11
  2.2 0.1 reshape.30.idr_ref
  2.3 2.3 %reshape.31.eo_ref = bf16[256,1536]{1,0:T(8,128)(2,1)S(1)} reshape(bf16[1,4,32,2,1536]{4,3,2,1,0:T(2,128)(2,1)} %param.10) | data formatting | bytes 1572864 | tf_op jit(solution)/shard_map/reshape | solution.py:665
  4.6 0.0 copy-start
  4.6 0.0 copy-start.1
  4.6 0.0 copy-start.2
  4.7 4.2 %reshape.32.hid_ref = bf16[256,4096]{1,0:T(8,128)(2,1)} reshape(bf16[1,4,32,2,4096]{4,3,2,1,0:T(2,128)(2,1)} %param.11) | data formatting | bytes 4194304 | tf_op jit(solution)/shard_map/reshape | solution.py:666
  8.8 0.0 copy-done
  8.8 0.0 copy-done.1
  8.8 0.0 copy-done.2
  8.8 125.7 %shard_map.85 = (bf16[128,1536]{1,0:T(8,128)(2,1)S(1)}, bf16[512,1536]{1,0:T(8,128)(2,1)S(1)}, f32[8,128]{1,0:T(8,128)S(1)}) custom-call(bf16[4,32,1536]{2,1,0:T(8,128)(2,1)S(1)} %copy-done, bf16[128,1536]{1,0:T(8,128)(2,1)S(1)} %bitcast.18, f32[8,3072]{1,0:T(8,128)S(1)} %bitcast.19, s32[1,256]{1,0:T(1,128)S(1)} %reshape.30.idr_ref, f32[2,128]{1,0:T(2,128)S(1)} %bitcast.17, ...), custom_call_target="tpu_custom_call" | custom-call | flops 8000000000 | bytes 8000000 | tf_op jit(solution)/shard_map/pallas_call | solution.py:645
  134.6 0.6 slice_bitcast_fusion
  135.2 0.7 copy.15
  135.9 1.1 copy.16
  (1 shorter events, 0.0 us)
Async XLA Ops:
  4.6 4.2 %copy-start = (bf16[4,32,1536]{2,1,0:T(8,128)(2,1)S(1)}, bf16[4,32,1536]{2,1,0:T(8,128)(2,1)}, u32[]{:S(2)}) copy-start(bf16[4,32,1536]{2,1,0:T(8,128)(2,1)} %top_ref.1) | copy-start | bytes 1179652
  4.6 4.2 %copy-start.1 = (bf16[1,4,32,1536]{3,2,1,0:T(8,128)(2,1)S(1)}, bf16[1,4,32,1536]{3,2,1,0:T(8,128)(2,1)}, u32[]{:S(2)}) copy-start(bf16[1,4,32,1536]{3,2,1,0:T(8,128)(2,1)} %param.7) | copy-start | bytes 1179652
  4.6 4.2 %copy-start.2 = (f32[1,3072,8]{1,2,0:T(8,128)S(1)}, f32[1,3072,8]{1,2,0:T(8,128)}, u32[]{:S(2)}) copy-start(f32[1,3072,8]{1,2,0:T(8,128)} %param.8) | copy-start | bytes 294916

commit v3 on v2

--- a/solution.py
+++ b/solution.py
@@ -56,9 +56,9 @@
 
 
 def kernel(
-    top_ref, x_ref, w_ref, idr_ref, idt_ref, eo_ref, hid_ref,
+    top_ref, x_ref, w_ref, ids_ref, eo_ref, hid_ref,
     cot_ref, down_ref, router_ref,
-    wb, pr, sm, szr, sg, ry, ryr, rz, rzr, topb, pick, hs, hy, hz, perm, seg, wq, xs, rel, sc, acc,
+    wb, pr, sm, szr, sg, ry, ryr, rz, rzr, topb, pick, hs, hy, hz, perm, seg, wq, xs, rel, sc, acc, hv, hv_sem,
     w_s, w_r, p_s, p_r, tz_s, tz_r, ring_s, ring_r, sz_s, sz_r, sy_s, sy_r, ry_s, ry_r, rz_s, rz_r,
     hy_s, hy_r, hz_s, hz_r, hf_s, xx_s, xx_r, rr_s, rr_r, cc_s, cc_r,
 ):
@@ -108,8 +108,21 @@
         for cc in range(2):
             greet((x, y * SIDE + (z + k) % SIDE, cc))
 
-    ids_row = idr_ref[...]
-    named = (jnp.broadcast_to(ids_row, (8, 256)) == iota((8, 256), 0)).astype(F32)
+    load = pltpu.make_async_copy(hid_ref, hv, hv_sem.at[0])
+    load.start()
+
+    ids = ids_ref[...].astype(F32).astype(BF16)
+    route = iota((8, 256), 1)
+    spread = (jnp.right_shift(iota((TOK, 256), 1), 1) & (TOK - 1)) == iota((TOK, 256), 0)
+    wide = jnp.dot(ids, jnp.where(spread, 1.0, 0.0).astype(BF16), preferred_element_type=F32)
+    own_row = iota((8, 256), 0) == 2 * jnp.right_shift(route, 6) + (route & 1)
+    ids_row = jnp.sum(jnp.where(own_row, wide, 0.0), axis=0, keepdims=True)
+    spread = (iota((TOK, 128), 1) & (TOK - 1)) == iota((TOK, 128), 0)
+    wide = jnp.dot(ids, jnp.where(spread, 1.0, 0.0).astype(BF16), preferred_element_type=F32)
+    first_row = iota((8, 128), 0) - 2 * jnp.right_shift(iota((8, 128), 1), 5)
+    ids_first = jnp.sum(jnp.where(first_row == 0, wide, 0.0), axis=0, keepdims=True)
+    ids_second = jnp.sum(jnp.where(first_row == 1, wide, 0.0), axis=0, keepdims=True)
+    named = (jnp.broadcast_to(ids_row, (8, 256)) == iota((8, 256), 0).astype(F32)).astype(F32)
     rank = jnp.dot(named.astype(BF16), earlier(6), preferred_element_type=F32)
     r48 = iota((48, 256), 0)
     m48 = divided(r48, CAP)
@@ -156,12 +169,13 @@
         topb[y, z] = top_ref[x, :, pl.ds(pl.multiple_of(c * quarter, 128), quarter)]
 
     def hidden_block(f, carry):
-        cols = hid_ref[:, pl.ds(pl.multiple_of(f * 512, 512), 512)]
+        cols = hv[:, :, pl.ds(pl.multiple_of(f * 512, 512), 512)].reshape(256, 512)
         got = jnp.dot(pick[...], cols, preferred_element_type=F32).astype(BF16)
         for e in range(WINDOW):
             hs[2 * e + f // 4, f % 4] = got[e * 48:(e + 1) * 48]
         return carry
 
+    load.wait()
     lax.fori_loop(0, 8, hidden_block, 0)
 
     def hy_copy(i):
@@ -185,7 +199,7 @@
     lax.fori_loop(0, SIDE, tz_wait, 0)
     ring_copy(y, 0, SIDE, 1, 1).start()
     ring_copy(y, 0, SIDE, 2, SIDE - 1).start()
-    lax.fori_loop(1, 3, hy_start, 0)
+    lax.fori_loop(1, 5, hy_start, 0)
     hy[y] = hs[y]
 
     pair = z // 2
@@ -232,14 +246,15 @@
     core_cols = pl.ds(pl.multiple_of(c * half, 128), half)
     inputs = x_ref[...]
     top_tokens = top_ref[...].reshape(MICRO * TOK, half)
-    outs = eo_ref[...]
+    outs = eo_ref[...].reshape(256, half)
     r128, c256 = iota((128, 256), 0), iota((128, 256), 1)
     pairs = jnp.where(c256 == 2 * r128, 1.0, jnp.where(c256 == 2 * r128 + 1, -1.0, 0.0))
     pr[x, c, 0:8] = by_parts(w_ref[:, core_cols], inputs, 1)
     products = contract(top_tokens, outs, 1, 1)
     dots = jnp.sum(products * jnp.abs(pairs), axis=0, keepdims=True)
-    pr[x, c, 8:16] = contract(jnp.broadcast_to(dots, (8, 256)), pairs, 1, 1, HIGHEST)
-    pr[x, c, 9:11] = idt_ref[...]
+    dots = contract(jnp.broadcast_to(dots, (8, 256)), pairs, 1, 1, HIGHEST)
+    lines = iota((8, 128), 0)
+    pr[x, c, 8:16] = jnp.where(lines == 1, ids_first, jnp.where(lines == 2, ids_second, dots))
 
     def w_wait(k):
         copy(w_ref, wb.at[(x + SECTIONS - k) % SECTIONS], w_s.at[k - 1], w_r.at[k - 1], at_x(k)).wait_recv()
@@ -326,9 +341,9 @@
         def _():
             ring_copy(source(i), 4, 4, SIDE - 1, SIDE - 1).start()
 
-        @pl.when(i < SIDE - 2)
-        def _():
-            hy_copy(i + 2).start()
+        @pl.when(i < 4)
+        def _():
+            hy_copy(i + 4).start()
 
     own_dl = jnp.zeros((8, 128), F32)
     for l in range(SECTIONS):
@@ -346,11 +361,6 @@
         ry_copy(k).start()
     ryr[y] = ry[y]
 
-    def first_rings(i, carry):
-        take_ring(i)
-        return carry
-
-    lax.fori_loop(1, 3, first_rings, 0)
 
     for k in range(1, SIDE):
         part = szr.at[(z + SIDE - k) % SIDE]
@@ -365,6 +375,12 @@
 
     for i in range(1, SIDE):
         sy_copy(i).start()
+
+    def first_rings(i, carry):
+        take_ring(i)
+        return carry
+
+    lax.fori_loop(1, 3, first_rings, 0)
 
     def rz_copy(k):
         zd = (z + k) % SIDE
@@ -627,6 +643,8 @@
         pltpu.VMEM((SIDE, 2, SIDE * CAP // 2, quarter), BF16),
         pltpu.VMEM((2, SIDE, SECTIONS, SIDE * CAP, quarter), BF16),
         pltpu.VMEM((tile, half), F32),
+        pltpu.VMEM((tokens, 2, half_ff), BF16),
+        dma((1,)),
         dma((3,)), dma((3,)),
         dma((7,)), dma((7,)),
         dma((4, 2)), dma((SIDE,)),
@@ -649,7 +667,7 @@
             jax.ShapeDtypeStruct((tile, half), BF16),
             jax.ShapeDtypeStruct((EXPERTS, 128), F32),
         ),
-        in_specs=[vmem] * 7,
+        in_specs=[vmem] * 5 + [pl.BlockSpec(memory_space=pl.ANY)],
         out_specs=(vmem, vmem, vmem),
         scratch_shapes=scratch,
         compiler_params=pltpu.CompilerParams(
@@ -660,10 +678,9 @@
         top_cotangent,
         layer_inputs.reshape(tokens, half),
         router_weight[0].T,
-        expert_ids.reshape(1, tokens * 2),
-        expert_ids.reshape(tokens, 2).T.astype(F32),
-        expert_outputs.reshape(tokens * 2, half),
-        hidden.reshape(tokens * 2, half_ff),
+        expert_ids[0].transpose(0, 2, 1).reshape(micro * 2, tok),
+        expert_outputs.reshape(tokens, 2, half),
+        hidden.reshape(tokens, 2, half_ff),
     )
     return (
         cotangent.reshape(1, micro, tok, half),

time: 137 us -> 130 us (0.949)
  Pallas kernels: 126 us -> 122 us
  local copies, waits for them, and re-layouts: 9.95 us -> 7.18 us
    reshape x3 -> x0, local copies, waits for them, and re-layouts: 6.58 us -> none  [the longest x1 4.16 us: per_device(): hidden.reshape(tokens * 2, half_ff)]
    unnamed x9 -> x12, local copies, waits for them, and re-layouts: 2.69 us -> 6.58 us
    pallas_call x1, Pallas kernels: 126 us -> 122 us  [per_device(): pl.pallas_call(kernel, out_shape=(jax.ShapeDtypeStruct((tokens, half), BF...]
where the time goes in v3:
time: 130 us
  Pallas kernels  122 us (94%)
  local copies, waits for them, and re-layouts  7.18 us (6%)
    pallas_call x1, Pallas kernels, per_device(): pl.pallas_call(kernel, out_shape=(jax.ShapeDtypeStruct((tokens, half), BF...  122 us
    unnamed x12, local copies, waits for them, and re-layouts  6.58 us

profile of v3, /device:TPU:1, one launch (start us, length us, event | category | flops | bytes accessed | tf_op | source)
XLA Modules:
  0.0 130.0 jit_solution(13152292766915623717)
XLA Ops:
  0.6 0.0 copy-start
  0.6 1.1 copy-done
  1.8 0.0 copy-start.1
  1.8 1.0 copy-done.1
  2.8 0.0 copy-start.2
  2.8 1.0 copy-done.2
  3.8 0.0 copy-start.3
  3.8 0.9 copy-done.3
  4.7 0.0 copy-start.4
  4.7 0.7 copy-done.4
  5.3 122.2 %shard_map.85 = (bf16[128,1536]{1,0:T(8,128)(2,1)S(1)}, bf16[512,1536]{1,0:T(8,128)(2,1)S(1)}, f32[8,128]{1,0:T(8,128)S(1)}) custom-call(bf16[4,32,1536]{2,1,0:T(8,128)(2,1)S(1)} %copy-done.1, bf16[128,1536]{1,0:T(8,128)(2,1)S(1)} %bitcast.20, f32[8,3072]{1,0:T(8,128)S(1)} %bitcast.21, s32[8,32]{1,0:T(8,128)S(1)} %bitcast.22, ...), custom_call_target="tpu_custom_call" | custom-call | flops 8000000000 | bytes 8000000 | tf_op jit(solution)/shard_map/pallas_call | solution.py:663
  127.5 0.6 slice_bitcast_fusion
  128.1 0.7 copy.11
  128.8 1.1 copy.12
Async XLA Ops:
  0.6 1.1 copy-start
  1.8 1.0 copy-start.1
  2.8 1.0 copy-start.2
  3.8 0.9 copy-start.3
  4.7 0.7 copy-start.4

commit v4 on v3

--- a/solution.py
+++ b/solution.py
@@ -58,7 +58,7 @@
 def kernel(
     top_ref, x_ref, w_ref, ids_ref, eo_ref, hid_ref,
     cot_ref, down_ref, router_ref,
-    wb, pr, sm, szr, sg, ry, ryr, rz, rzr, topb, pick, hs, hy, hz, perm, seg, wq, xs, rel, sc, acc, hv, hv_sem,
+    wb, pr, sm, szr, sg, ry, ryr, rz, rzr, topb, pick, hs, hy, hz, perm, seg, wq, xs, rel, sc, acc, hv, tv, xv, ev, iv, in_sem,
     w_s, w_r, p_s, p_r, tz_s, tz_r, ring_s, ring_r, sz_s, sz_r, sy_s, sy_r, ry_s, ry_r, rz_s, rz_r,
     hy_s, hy_r, hz_s, hz_r, hf_s, xx_s, xx_r, rr_s, rr_r, cc_s, cc_r,
 ):
@@ -108,10 +108,17 @@
         for cc in range(2):
             greet((x, y * SIDE + (z + k) % SIDE, cc))
 
-    load = pltpu.make_async_copy(hid_ref, hv, hv_sem.at[0])
-    load.start()
-
-    ids = ids_ref[...].astype(F32).astype(BF16)
+    loads = [
+        pltpu.make_async_copy(src, dst, in_sem.at[n])
+        for n, (src, dst) in enumerate(
+            ((ids_ref, iv), (hid_ref, hv), (w_ref, wb.at[x]), (top_ref, tv), (x_ref, xv), (eo_ref, ev))
+        )
+    ]
+    for load in loads:
+        load.start()
+
+    loads[0].wait()
+    ids = iv[...].astype(F32).astype(BF16)
     route = iota((8, 256), 1)
     spread = (jnp.right_shift(iota((TOK, 256), 1), 1) & (TOK - 1)) == iota((TOK, 256), 0)
     wide = jnp.dot(ids, jnp.where(spread, 1.0, 0.0).astype(BF16), preferred_element_type=F32)
@@ -143,7 +150,6 @@
 
     for k in range(1, SECTIONS):
         w_copy(k).start()
-    wb[x] = w_ref[...]
 
     tilt = (z + c) % 2
     local = tilt == 0
@@ -164,9 +170,11 @@
             else:
                 tz_copy(r, cc).start()
 
+    loads[3].wait()
+
     @pl.when(local)
     def _():
-        topb[y, z] = top_ref[x, :, pl.ds(pl.multiple_of(c * quarter, 128), quarter)]
+        topb[y, z] = tv[x, :, pl.ds(pl.multiple_of(c * quarter, 128), quarter)]
 
     def hidden_block(f, carry):
         cols = hv[:, :, pl.ds(pl.multiple_of(f * 512, 512), 512)].reshape(256, 512)
@@ -175,7 +183,7 @@
             hs[2 * e + f // 4, f % 4] = got[e * 48:(e + 1) * 48]
         return carry
 
-    load.wait()
+    loads[1].wait()
     lax.fori_loop(0, 8, hidden_block, 0)
 
     def hy_copy(i):
@@ -199,7 +207,7 @@
     lax.fori_loop(0, SIDE, tz_wait, 0)
     ring_copy(y, 0, SIDE, 1, 1).start()
     ring_copy(y, 0, SIDE, 2, SIDE - 1).start()
-    lax.fori_loop(1, 5, hy_start, 0)
+    lax.fori_loop(1, 3, hy_start, 0)
     hy[y] = hs[y]
 
     pair = z // 2
@@ -244,12 +252,14 @@
     send_hidden(0)
 
     core_cols = pl.ds(pl.multiple_of(c * half, 128), half)
-    inputs = x_ref[...]
-    top_tokens = top_ref[...].reshape(MICRO * TOK, half)
-    outs = eo_ref[...].reshape(256, half)
+    for load in (loads[2], loads[4], loads[5]):
+        load.wait()
+    inputs = xv[...]
+    top_tokens = tv[...].reshape(MICRO * TOK, half)
+    outs = ev[...].reshape(256, half)
     r128, c256 = iota((128, 256), 0), iota((128, 256), 1)
     pairs = jnp.where(c256 == 2 * r128, 1.0, jnp.where(c256 == 2 * r128 + 1, -1.0, 0.0))
-    pr[x, c, 0:8] = by_parts(w_ref[:, core_cols], inputs, 1)
+    pr[x, c, 0:8] = by_parts(wb[x, :, core_cols], inputs, 1)
     products = contract(top_tokens, outs, 1, 1)
     dots = jnp.sum(products * jnp.abs(pairs), axis=0, keepdims=True)
     dots = contract(jnp.broadcast_to(dots, (8, 256)), pairs, 1, 1, HIGHEST)
@@ -341,9 +351,13 @@
         def _():
             ring_copy(source(i), 4, 4, SIDE - 1, SIDE - 1).start()
 
-        @pl.when(i < 4)
-        def _():
-            hy_copy(i + 4).start()
+        @pl.when(i < 5)
+        def _():
+            hy_copy(i + 2).start()
+
+        @pl.when(i == 4)
+        def _():
+            hy_copy(SIDE - 1).start()
 
     own_dl = jnp.zeros((8, 128), F32)
     for l in range(SECTIONS):
@@ -361,6 +375,12 @@
         ry_copy(k).start()
     ryr[y] = ry[y]
 
+    def first_rings(i, carry):
+        take_ring(i)
+        return carry
+
+    lax.fori_loop(1, 3, first_rings, 0)
+
 
     for k in range(1, SIDE):
         part = szr.at[(z + SIDE - k) % SIDE]
@@ -376,11 +396,6 @@
     for i in range(1, SIDE):
         sy_copy(i).start()
 
-    def first_rings(i, carry):
-        take_ring(i)
-        return carry
-
-    lax.fori_loop(1, 3, first_rings, 0)
 
     def rz_copy(k):
         zd = (z + k) % SIDE
@@ -535,7 +550,7 @@
         def _():
             small_wait(i)
 
-        @pl.when(i < SIDE)
+        @pl.when((i >= 1) & (i < SIDE))
         def _():
             select(i)
 
@@ -569,6 +584,7 @@
 
         return carry
 
+    select(0)
     lax.fori_loop(0, SIDE + 3, body, 0)
     down_ref[...] = acc[...].astype(BF16)
     for k in range(1, SIDE):
@@ -644,7 +660,11 @@
         pltpu.VMEM((2, SIDE, SECTIONS, SIDE * CAP, quarter), BF16),
         pltpu.VMEM((tile, half), F32),
         pltpu.VMEM((tokens, 2, half_ff), BF16),
-        dma((1,)),
+        pltpu.VMEM((micro, tok, half), BF16),
+        pltpu.VMEM((tokens, half), BF16),
+        pltpu.VMEM((tokens, 2, half), BF16),
+        pltpu.VMEM((2 * micro, tok), jnp.int32),
+        dma((6,)),
         dma((3,)), dma((3,)),
         dma((7,)), dma((7,)),
         dma((4, 2)), dma((SIDE,)),
@@ -667,11 +687,11 @@
             jax.ShapeDtypeStruct((tile, half), BF16),
             jax.ShapeDtypeStruct((EXPERTS, 128), F32),
         ),
-        in_specs=[vmem] * 5 + [pl.BlockSpec(memory_space=pl.ANY)],
+        in_specs=[pl.BlockSpec(memory_space=pl.ANY)] * 6,
         out_specs=(vmem, vmem, vmem),
         scratch_shapes=scratch,
         compiler_params=pltpu.CompilerParams(
-            collective_id=0, has_side_effects=True, vmem_limit_bytes=50 * 1024 * 1024
+            collective_id=0, has_side_effects=True, vmem_limit_bytes=58 * 1024 * 1024
         ),
         cost_estimate=pl.CostEstimate(flops=8_000_000_000, bytes_accessed=8_000_000, transcendentals=0),
     )(

time: 130 us -> 140 us (1.077)
  Pallas kernels: 122 us -> 133 us
  local copies, waits for them, and re-layouts: 7.18 us -> 5.68 us
    pallas_call x1, Pallas kernels: 122 us -> 133 us  [per_device(): pl.pallas_call(kernel, out_shape=(jax.ShapeDtypeStruct((tokens, half), BF...]
    unnamed x12 -> x2, local copies, waits for them, and re-layouts: 6.58 us -> 4.42 us
where the time goes in v4:
time: 140 us; the launch traced here: 139 us
  Pallas kernels  133 us (95%)
  local copies, waits for them, and re-layouts  5.68 us (4%)
    pallas_call x1, Pallas kernels, per_device(): pl.pallas_call(kernel, out_shape=(jax.ShapeDtypeStruct((tokens, half), BF...  133 us
    unnamed x2, local copies, waits for them, and re-layouts  4.42 us

profile of v4, /device:TPU:1, one launch (start us, length us, event | category | flops | bytes accessed | tf_op | source)
XLA Modules:
  0.0 139.3 jit_solution(13045828874986231634)
XLA Ops:
  0.6 133.0 %shard_map.85 = (bf16[128,1536]{1,0:T(8,128)(2,1)}, bf16[512,1536]{1,0:T(8,128)(2,1)}, f32[8,128]{1,0:T(8,128)}) custom-call(bf16[4,32,1536]{2,1,0:T(8,128)(2,1)} %top_ref.1, bf16[128,1536]{1,0:T(8,128)(2,1)} %bitcast.21, f32[8,3072]{1,0:T(8,128)} %bitcast.22, s32[8,32]{1,0:T(8,128)} %bitcast.23, bf16[128,2,1536]{2,1,0:T(2,128)(2,1)} %bitcast.20, ...), custom_call_target="tpu_custom_call" | custom-call | flops 8000000000 | bytes 8000000 | tf_op jit(solution)/shard_map/pallas_call | solution.py:683
  133.6 1.3 slice_bitcast_fusion
  134.9 1.8 %copy.11 = bf16[1,4,32,1536]{3,2,1,0:T(8,128)(2,1)} copy(bf16[1,4,32,1536]{3,2,1,0:T(8,128)(2,1)} %bitcast.18) | data formatting | bytes 786432
  136.7 2.7 %copy.12 = bf16[1,1,1,512,1536]{4,3,2,1,0:T(8,128)(2,1)} copy(bf16[1,1,1,512,1536]{4,3,2,1,0:T(8,128)(2,1)} %bitcast.17) | data formatting | bytes 3145728

commit v5 on v3

--- a/solution.py
+++ b/solution.py
@@ -199,7 +199,7 @@
     lax.fori_loop(0, SIDE, tz_wait, 0)
     ring_copy(y, 0, SIDE, 1, 1).start()
     ring_copy(y, 0, SIDE, 2, SIDE - 1).start()
-    lax.fori_loop(1, 5, hy_start, 0)
+    lax.fori_loop(1, SIDE, hy_start, 0)
     hy[y] = hs[y]
 
     pair = z // 2
@@ -340,10 +340,6 @@
         @pl.when(i == 6)
         def _():
             ring_copy(source(i), 4, 4, SIDE - 1, SIDE - 1).start()
-
-        @pl.when(i < 4)
-        def _():
-            hy_copy(i + 4).start()
 
     own_dl = jnp.zeros((8, 128), F32)
     for l in range(SECTIONS):

time: 130 us -> 136 us (1.046)
  Pallas kernels: 122 us -> 128 us
    pallas_call x1, Pallas kernels: 122 us -> 128 us  [per_device(): pl.pallas_call(kernel, out_shape=(jax.ShapeDtypeStruct((tokens, half), BF...]
where the time goes in v5:
time: 136 us; the launch traced here: 135 us
  Pallas kernels  128 us (94%)
  local copies, waits for them, and re-layouts  7.18 us (5%)
    pallas_call x1, Pallas kernels, per_device(): pl.pallas_call(kernel, out_shape=(jax.ShapeDtypeStruct((tokens, half), BF...  128 us
    unnamed x12, local copies, waits for them, and re-layouts  6.58 us

profile of v5, /device:TPU:1, one launch (start us, length us, event | category | flops | bytes accessed | tf_op | source)
XLA Modules:
  0.0 135.4 jit_solution(4438263912759251799)
XLA Ops:
  0.6 0.0 copy-start
  0.6 1.1 copy-done
  1.8 0.0 copy-start.1
  1.8 1.0 copy-done.1
  2.8 0.0 copy-start.2
  2.8 1.0 copy-done.2
  3.8 0.0 copy-start.3
  3.8 0.9 copy-done.3
  4.7 0.0 copy-start.4
  4.7 0.7 copy-done.4
  5.3 127.6 %shard_map.85 = (bf16[128,1536]{1,0:T(8,128)(2,1)S(1)}, bf16[512,1536]{1,0:T(8,128)(2,1)S(1)}, f32[8,128]{1,0:T(8,128)S(1)}) custom-call(bf16[4,32,1536]{2,1,0:T(8,128)(2,1)S(1)} %copy-done.1, bf16[128,1536]{1,0:T(8,128)(2,1)S(1)} %bitcast.20, f32[8,3072]{1,0:T(8,128)S(1)} %bitcast.21, s32[8,32]{1,0:T(8,128)S(1)} %bitcast.22, ...), custom_call_target="tpu_custom_call" | custom-call | flops 8000000000 | bytes 8000000 | tf_op jit(solution)/shard_map/pallas_call | solution.py:659
  133.0 0.6 slice_bitcast_fusion
  133.6 0.7 copy.11
  134.3 1.1 copy.12
Async XLA Ops:
  0.6 1.1 copy-start
  1.8 1.0 copy-start.1
  2.8 1.0 copy-start.2
  3.8 0.9 copy-start.3
  4.7 0.7 copy-start.4
